TPU v7x, 32 devices: a whole 2x2x4 slice. The times are simulated.
32 devices in a mesh: groups: 2 (over y), seq: 4 (over z), tensor: 4 (over x, core).
Axes of the slice: x: 2, y: 2, z: 4, core: 2. Of those that a mesh axis runs over, the one named last changes fastest.
Arguments:
- text_states: bfloat16 [64, 8192], P(('groups', 'seq')), parts along dimension 0, may hold values from -18 to 18
- vision_states: bfloat16 [2048, 8192], P(('groups', 'seq'), 'tensor'), parts along dimension 0, may hold values from -6 to 6
- norm_gain: bfloat16 [8192], replicated, may hold values from 0.25 to 1.75
- query_weight: bfloat16 [8192, 8192], P('seq', 'tensor'), may hold values from -0.0625 to 0.0625
- key_value_weight: bfloat16 [2, 8192, 1024], P(None, 'tensor', 'seq'), may hold values from -0.0625 to 0.0625
- out_weight: bfloat16 [8192, 8192], P('tensor', 'seq'), may hold values from -0.0625 to 0.0625
- query_gain: float32 [128], replicated, may hold values from 4.5 to 6
- key_norm_gain: float32 [128], replicated, may hold values from 4.5 to 6
- attn_gate: float32 [1], replicated, may hold values from 0.4 to 2
- tile_counts: int32 [4], P('groups'), parts along dimension 0, may hold values from 128 to 512, as said below
- tile_mask: int32 [2, 2], P('groups'), parts along dimension 0, may hold values from 0 to 1, as said below
Outputs:
- layer_out: bfloat16 [64, 8192], P(('groups', 'tensor'), 'seq'), parts along dimension 0
There are 2 independent parts, one for each index of `groups`. A program takes and returns all parts, laid end to end along the dimension named above; an argument that names none is the same for every part. Nothing has to cross between parts.
Inputs may be any that keep to these rules, and one draw needn't show every extreme that they name: `tile_counts`: some tile is full (512 valid tokens) and some tile holds exactly 128; valid tokens are the first slots of a tile. `tile_mask`: every row has at least one 1 and at least one 0.
All inputs are finite; a program needn't handle non-finite values.
Results may differ from a plain program's by a relative error of at most 0.0055.
The roundings to bfloat16 on the way count: a program that leaves them out, or rounds other values in their place, can miss the bound.
Values may be sent and summed in bfloat16 or wider, within the bound.
A program may use at most 128 MiB of HBM per device.

v0:
```python
import jax
import jax.numpy as jnp
from jax import lax
from jax.sharding import PartitionSpec as P

TILE_LEN = 512
TEXT_BLOCK = 32


EPS = 1e-05
NEG = -1e30


def combined_all(part, axis, combine):
    gathered = jax.tree.map(lambda a: lax.all_gather(a, axis), part)

    def take(source):
        return jax.tree.map(lambda a: lax.dynamic_index_in_dim(a, source, 0, False), gathered)

    return lax.fori_loop(
        1, lax.axis_size(axis), lambda source, state: combine(state, take(source)), take(0)
    )


def root_mean_rows(value_matrix, gain):
    mean_sq = jnp.mean(value_matrix * value_matrix, axis=-1, keepdims=True)
    return value_matrix * lax.rsqrt(mean_sq + EPS) * gain


def allowed_mask(query_count, key_start, key_count, tile_counts, tile_mask):
    tiles = tile_counts.shape[0]
    blocks = tile_mask.shape[0]
    key_pos = key_start + jnp.arange(key_count, dtype=jnp.int32)
    key_tile = key_pos // TILE_LEN
    tile_match = key_tile[:, None] == jnp.arange(tiles, dtype=jnp.int32)[None, :]
    count_here = jnp.sum(jnp.where(tile_match, tile_counts[None, :], 0), axis=1)
    slot_ok = key_pos % TILE_LEN < count_here
    query_pos = jnp.arange(query_count, dtype=jnp.int32)
    block_match = (
        query_pos[:, None] // TEXT_BLOCK == jnp.arange(blocks, dtype=jnp.int32)[None, :]
    ).astype(jnp.float32)
    row_tiles = jnp.dot(block_match, tile_mask.astype(jnp.float32), precision=lax.Precision.HIGHEST)
    seen = jnp.dot(row_tiles, tile_match.astype(jnp.float32).T, precision=lax.Precision.HIGHEST)
    return (seen > 0.5) & slot_ok[None, :]


def partial_attend(query_matrix, key_matrix, value_matrix, allowed):
    scale = query_matrix.shape[-1] ** (-0.5)
    scores = (
        jnp.einsum("ihgd,khd->ihgk", query_matrix, key_matrix, preferred_element_type=jnp.float32)
        * scale
    )
    mask = allowed[:, None, None, :]
    masked = jnp.where(mask, scores, NEG)
    top = jnp.max(masked, axis=-1)
    weights = jnp.where(mask, jnp.exp(masked - top[..., None]), 0.0)
    total = jnp.sum(weights, axis=-1)
    summed = jnp.einsum("ihgk,khd->ihgd", weights, value_matrix, precision=lax.Precision.HIGHEST)
    return (top, total, summed)


def join_parts(first, second):
    top = jnp.maximum(first[0], second[0])
    scale_first = jnp.exp(first[0] - top)
    scale_second = jnp.exp(second[0] - top)
    total = first[1] * scale_first + second[1] * scale_second
    summed = first[2] * scale_first[..., None] + second[2] * scale_second[..., None]
    return (top, total, summed)


def local(
    text_states,
    vision_states,
    norm_gain,
    query_weight,
    key_value_weight,
    out_weight,
    query_gain,
    key_norm_gain,
    attn_gate,
    tile_counts,
    tile_mask,
):
    seq_count = lax.axis_size("seq")
    seq_index = lax.axis_index("seq")
    tensor_count = lax.axis_size("tensor")
    tensor_index = lax.axis_index("tensor")
    text_dev = text_states.shape[0]
    text_all = text_dev * seq_count
    vis_dev = vision_states.shape[0]
    head_size = query_gain.shape[0]
    query_local = query_weight.shape[1] // head_size
    normed = root_mean_rows(text_states.astype(jnp.float32), norm_gain.astype(jnp.float32)).astype(
        jnp.bfloat16
    )
    raw_cols, normed_cols = (
        lax.all_to_all(text_states, "seq", split_axis=1, concat_axis=0, tiled=True),
        lax.all_to_all(normed, "seq", split_axis=1, concat_axis=0, tiled=True),
    )
    rows = normed_cols
    query_raw = lax.psum_scatter(
        jnp.dot(rows, query_weight, preferred_element_type=jnp.float32),
        "seq",
        scatter_dimension=0,
        tiled=True,
    )
    query_matrix = root_mean_rows(
        query_raw.reshape(text_dev, query_local, head_size), query_gain
    ).astype(jnp.bfloat16)
    kv_full = jnp.einsum(
        "vd,jdc->jvc",
        vision_states,
        lax.all_gather(key_value_weight, "seq", axis=2, tiled=True),
        preferred_element_type=jnp.float32,
    )
    kv_local = lax.psum_scatter(kv_full, "tensor", scatter_dimension=2, tiled=True)
    kv_heads = kv_local.shape[2] // head_size
    group_size = query_local // kv_heads
    key_matrix = root_mean_rows(
        kv_local[0].reshape(vis_dev, kv_heads, head_size), key_norm_gain
    ).astype(jnp.bfloat16)
    value_matrix = kv_local[1].astype(jnp.bfloat16).reshape(vis_dev, kv_heads, head_size)
    queries_grouped = query_matrix.reshape(text_dev, kv_heads, group_size, head_size)
    query_all = lax.all_gather(queries_grouped, "seq", axis=0, tiled=True)
    allowed = allowed_mask(text_all, seq_index * vis_dev, vis_dev, tile_counts, tile_mask)
    local_parts = partial_attend(query_all, key_matrix, value_matrix.astype(jnp.float32), allowed)
    top, total, summed = combined_all(local_parts, "seq", join_parts)
    attention_all = (
        (summed / total[..., None]).reshape(text_all, query_local * head_size).astype(jnp.bfloat16)
    )
    rows_out = text_all // tensor_count
    rows = attention_all
    branch = lax.psum_scatter(
        jnp.dot(rows, out_weight, preferred_element_type=jnp.float32),
        "tensor",
        scatter_dimension=0,
        tiled=True,
    )
    residual = lax.dynamic_slice_in_dim(raw_cols, tensor_index * rows_out, rows_out, 0)
    return (residual.astype(jnp.float32) + jnp.tanh(attn_gate[0]) * branch).astype(jnp.bfloat16)


def solution(mesh):
    return jax.shard_map(
        local,
        mesh=mesh,
        in_specs=(
            P(("groups", "seq"), None),
            P(("groups", "seq"), "tensor"),
            P(),
            P("seq", "tensor"),
            P(None, "tensor", "seq"),
            P("tensor", "seq"),
            P(),
            P(),
            P(),
            P("groups"),
            P("groups", None),
        ),
        out_specs=P(("groups", "tensor"), "seq"),
        check_vma=False,
    )
```

profile of v0, /device:TPU:0, one launch (start us, length us, event | category | flops | bytes accessed | tf_op | source)
XLA Modules:
  0.0 289.4 jit_solution(2777696798040319785)
XLA Ops:
  6.5 4.1 %copy.87 = bf16[2,2048,256]{1,2,0:T(8,128)(2,1)} copy(bf16[2,2048,256]{2,1,0:T(8,128)(2,1)} %param.17) | data formatting | bytes 4194304 | tf_op args[4]
  10.7 0.7 convert_element_type.43
  11.4 1.1 fusion.9
  12.5 1.0 fusion.11
  13.5 12.2 %all_to_all.38 = bf16[8,4,2048]{2,0,1:T(8,128)(2,1)S(1)} all-to-all(bf16[8,4,2048]{2,0,1:T(8,128)(2,1)S(1)} %bitcast.84), channel_id=1, replica_groups=mesh['groups'=2,'seq'=4,'tensor'=4] {'seq'}, dimensions={1} | all-to-all | bytes 262144 | tf_op jit(solution)/shard_map/all_to_all | solution.py:98
  25.7 5.9 %fusion.20 = f32[32,2048]{1,0:T(8,128)} fusion(bf16[2048,2048]{1,0:T(8,128)(2,1)} %param.16, bf16[8,4,2048]{2,0,1:T(8,128)(2,1)S(1)} %all_to_all.38), kind=kOutput, calls=%fused_computation.36 | convolution fusion | flops 268435456 | bytes 8781824 | tf_op jit(solution)/shard_map/dot_general | solution.py:102
  31.8 131.4 %all-gather.6.cloned.1.call-done = bf16[2,2048,1024]{1,2,0:T(8,128)(2,1)} async-done(((bf16[2,2048,256]{1,2,0:T(8,128)(2,1)}), bf16[2,2048,1024]{1,2,0:T(8,128)(2,1)}) %all-gather.6.cloned.1.call-update) | async-done | bytes 8388624 | tf_op jit(solution)/shard_map/all_gather | solution.py:113
  163.2 7.2 %convolution_bitcast_fusion = f32[2,256,1024]{1,2,0:T(8,128)} fusion(bf16[2,2048,1024]{1,2,0:T(8,128)(2,1)} %all-gather.6.cloned.1.call-done, bf16[256,2048]{1,0:T(8,128)(2,1)S(1)} %copy-done), kind=kOutput, calls=%fused_computation.10 | convolution fusion | flops 2147483648 | bytes 11534336 | tf_op jit(solution)/shard_map/vd,jdc->jvc/dot_general | solution.py:110
  170.4 0.1 select_reduce_fusion
  170.5 0.2 fusion.6
  170.8 12.5 %reduce-scatter.6.cloned.1.call-done = f32[8,2048]{1,0:T(8,128)} async-done(((f32[32,2048]{1,0:T(8,128)}), f32[8,2048]{1,0:T(8,128)}) %reduce-scatter.6.cloned.1.call-update) | async-done | bytes 65552 | tf_op jit(solution)/shard_map/reduce_scatter | solution.py:101
  183.3 0.9 bitcast_reduce_fusion
  184.4 0.9 multiply_convert_fusion.1
  185.3 12.3 %all_gather.25 = bf16[32,2,8,128]{3,0,2,1:T(8,128)(2,1)S(1)} all-gather(bf16[8,2,8,128]{3,0,2,1:T(8,128)(2,1)S(1)} %multiply_convert_fusion.1), channel_id=1, replica_groups=mesh['groups'=2,'seq'=4,'tensor'=4] {'seq'}, dimensions={0}, use_global_device_ids=true | all-gather | bytes 163840 | tf_op jit(solution)/shard_map/all_gather | solution.py:124
  197.6 18.1 %reduce-scatter.4.cloned.1.call-done = f32[2,256,256]{1,2,0:T(8,128)} async-done(((f32[2,256,1024]{1,2,0:T(8,128)}), f32[2,256,256]{1,2,0:T(8,128)}) %reduce-scatter.4.cloned.1.call-update) | async-done | bytes 524304 | tf_op jit(solution)/shard_map/reduce_scatter | solution.py:116
  215.7 1.0 slice.15
  216.6 0.1 copy.88
  216.8 0.4 fusion.33
  217.2 1.0 slice.21
  218.2 1.2 convolution_bitcast_fusion.1
  219.5 0.1 copy.91
  219.6 0.3 fusion.8
  219.9 0.1 copy.92
  219.9 13.8 %all-gather.1 = f32[128,2,8]{2,1,0:T(2,128)S(1)} all-gather(f32[32,2,8]{2,1,0:T(2,128)S(1)} %copy.92), channel_id=3, replica_groups=mesh['groups'=2,'seq'=4,'tensor'=4] {'seq'}, dimensions={0}, use_global_device_ids=true | all-gather | bytes 10240 | tf_op jit(solution)/shard_map/all_gather | solution.py:15
  233.9 14.5 %all-gather = f32[128,2,8]{2,1,0:T(2,128)S(1)} all-gather(f32[32,2,8]{2,1,0:T(2,128)S(1)} %copy.91), channel_id=2, replica_groups=mesh['groups'=2,'seq'=4,'tensor'=4] {'seq'}, dimensions={0}, use_global_device_ids=true | all-gather | bytes 10240 | tf_op jit(solution)/shard_map/all_gather | solution.py:15
  248.5 2.2 all-gather.8.cloned.1.call-done
  250.7 1.0 slice.19
  251.7 0.2 copy.98
  251.9 4.5 %while.19 = (s32[]{:T(128)}, f32[32,2,8]{0,2,1:T(8,128)S(1)}, f32[32,2,8]{0,2,1:T(8,128)S(1)}, f32[32,2,8,128]{3,2,1,0:T(8,128)S(1)}, f32[4,32,2,8]{1,3,2,0:T(8,...) while((s32[]{:T(128)}, f32[32,2,8]{0,2,1:T(8,128)S(1)}, ...), condition=%wide.region_9.10_spmd, body=%wide.region_8.9_spmd.sunk | while | flops 199685 | bytes 1339543 | solution.py:20
  251.9 0.1 copy.127
  252.0 0.1 copy.128
  252.1 1.0 constant_dynamic-slice_fusion.2
  253.1 0.3 fusion.42
  253.4 0.1 copy.127
  253.5 0.1 copy.128
  253.6 1.0 constant_dynamic-slice_fusion.2
  254.6 0.3 fusion.42
  254.9 0.1 copy.127
  255.0 0.1 copy.128
  255.1 1.0 constant_dynamic-slice_fusion.2
  256.1 0.3 fusion.42
  256.4 0.1 copy.102
  256.5 0.1 divide_convert_fusion
  256.6 5.6 %fusion.17 = f32[32,2048]{1,0:T(8,128)} fusion(bf16[2048,2048]{1,0:T(8,128)(2,1)} %param.18, bf16[4,8,16,128]{3,2,1,0:T(8,128)(2,1)S(1)} %bitcast.80), kind=kOutput, calls=%fused_computation.33 | convolution fusion | flops 268435456 | bytes 8781824 | tf_op jit(solution)/shard_map/dot_general | solution.py:134
  262.3 3.3 %all-to-all-start = ((bf16[8,4,2048]{2,0,1:T(8,128)(2,1)}), bf16[8,4,2048]{2,0,1:T(8,128)(2,1)S(1)}, u32[]{:S(2)}, u32[]{:S(2)}) async-start(bf16[8,4,2048]{2,0,1:T(8,128)(2,1)} %bitcast.3), calls=%async_computation | async-start | bytes 262144 | tf_op jit(solution)/shard_map/all_to_all | solution.py:97
  266.3 5.5 %all-to-all-done = bf16[8,4,2048]{2,0,1:T(8,128)(2,1)S(1)} async-done(((bf16[8,4,2048]{2,0,1:T(8,128)(2,1)}), bf16[8,4,2048]{2,0,1:T(8,128)(2,1)S(1)}, u32[]{:S(2)}, u32[]{:S(2)}) %all-to-all-start) | async-done | bytes 131104 | tf_op jit(solution)/shard_map/all_to_all | solution.py:97
  271.9 9.6 %reduce-scatter.8.cloned.1.call-done = f32[8,2048]{1,0:T(8,128)} async-done(((f32[32,2048]{1,0:T(8,128)}), f32[8,2048]{1,0:T(8,128)}) %reduce-scatter.8.cloned.1.call-update) | async-done | bytes 65552 | tf_op jit(solution)/shard_map/reduce_scatter | solution.py:133
  281.4 1.5 add_convert_fusion
  (39 shorter events, 0.9 us)
Async XLA Ops:
  6.5 156.6 %copy-start = (bf16[256,2048]{1,0:T(8,128)(2,1)S(1)}, bf16[256,2048]{1,0:T(8,128)(2,1)}, u32[]{:S(2)}) copy-start(bf16[256,2048]{1,0:T(8,128)(2,1)} %param.14) | copy-start | bytes 3145732
  6.5 156.6 %all-gather.6.cloned.1.call-start = ((), (), s32[]{:S(2)}) async-start(), calls=%async_computation.5 | async-start | bytes 10485760 | tf_op jit(solution)/shard_map/all_gather | solution.py:113
  10.7 172.6 %reduce-scatter.6.cloned.1.call-start = ((), (), s32[]{:S(2)}) async-start(), calls=%async_computation.7 | async-start | bytes 327680 | tf_op jit(solution)/shard_map/reduce_scatter | solution.py:101
  31.7 138.8 %copy-start.3 = (s32[2]{0:T(128)S(1)}, s32[2]{0:T(128)}, u32[]{:S(2)}) copy-start(s32[2]{0:T(128)} %param.22) | copy-start | bytes 28
  31.7 138.9 %copy-start.4 = (s32[1,2]{1,0:T(1,128)S(1)}, s32[1,2]{1,0:T(1,128)}, u32[]{:S(2)}) copy-start(s32[1,2]{1,0:T(1,128)} %param.23) | copy-start | bytes 28
  31.7 152.7 %copy-start.1 = (f32[128]{0:T(128)S(1)}, f32[128]{0:T(128)}, u32[]{:S(2)}) copy-start(f32[128]{0:T(128)} %param.19) | copy-start | bytes 1540
  31.7 185.1 %copy-start.2 = (f32[128]{0:T(128)S(1)}, f32[128]{0:T(128)}, u32[]{:S(2)}) copy-start(f32[128]{0:T(128)} %param.20) | copy-start | bytes 1540
  31.7 184.0 %reduce-scatter.4.cloned.1.call-start = ((), (), s32[]{:S(2)}) async-start(), calls=%async_computation.6 | async-start | bytes 2621440 | tf_op jit(solution)/shard_map/reduce_scatter | solution.py:116
  170.3 80.4 %all-gather.8.cloned.1.call-start = ((), (), s32[]{:S(2)}) async-start(), calls=%async_computation.9 | async-start | bytes 1310720 | tf_op jit(solution)/shard_map/all_gather | solution.py:15
  219.4 62.0 %reduce-scatter.8.cloned.1.call-start = ((), (), s32[]{:S(2)}) async-start(), calls=%async_computation.8 | async-start | bytes 327680 | tf_op jit(solution)/shard_map/reduce_scatter | solution.py:133
  262.3 9.6 %all-to-all-start = ((bf16[8,4,2048]{2,0,1:T(8,128)(2,1)}), bf16[8,4,2048]{2,0,1:T(8,128)(2,1)S(1)}, u32[]{:S(2)}, u32[]{:S(2)}) async-start(bf16[8,4,2048]{2,0,1:T(8,128)(2,1)} %bitcast.3), calls=%async_computation | async-start | bytes 262144 | tf_op jit(solution)/shard_map/all_to_all | solution.py:97
Sparse Core Ops, SparseCore 0:
  10.8 152.3 all-gather.5
  165.4 17.8 reduce-scatter.5
  186.0 29.6 reduce-scatter.3
  219.6 31.1 all-gather.7
  262.4 18.9 reduce-scatter.7
where the time goes:
time: 290 us; the launch traced here: 289 us
  waiting for transfers between devices  179 us (62%)
  blocking collectives  52.7 us (18%)
  matrix products  20.5 us (7%)
  between operations  14 us (5%)
  local copies, waits for them, and re-layouts  11.5 us (4%)
  other arithmetic  7.69 us (3%)
  starting transfers between devices  3.51 us (1%)
    all_gather x1, waiting for transfers between devices, local(): lax.all_gather(key_value_weight, 'seq', axis=2, tiled=True)  131 us
    all_gather x2, blocking collectives, combined_all(): gathered = jax.tree.map(lambda a: lax.all_gather(a, axis), part)  28.2 us
    reduce_scatter x1, waiting for transfers between devices, local(): lax.psum_scatter(kv_full, 'tensor', scatter_dimension=2, tiled=True)  18.1 us
    reduce_scatter x1, waiting for transfers between devices, local(): lax.psum_scatter(jnp.dot(rows, query_weight, preferred_element_type=jnp.f...  12.5 us
    all_gather x1, blocking collectives, local(): query_all = lax.all_gather(queries_grouped, 'seq', axis=0, tiled=True)  12.3 us
    all_to_all x1, blocking collectives, local(): lax.all_to_all(normed, 'seq', split_axis=1, concat_axis=0, tiled=True)  12.2 us
    reduce_scatter x1, waiting for transfers between devices, local(): lax.psum_scatter(jnp.dot(rows, out_weight, preferred_element_type=jnp.flo...  9.56 us
    dot_general x1, matrix products, local(): jnp.einsum('vd,jdc->jvc', vision_states, lax.all_gather(key_value_weight,...  7.17 us
  transfers between devices with their start and end apart: 6, of which 6 were waited for; matrix products, arithmetic and copies ran while one was open for 7% of the time, Pallas kernels for 0%

commit v1 on v0

--- a/solution.py
+++ b/solution.py
@@ -1,6 +1,8 @@
 import jax
 import jax.numpy as jnp
 from jax import lax
+from jax.experimental import pallas as pl
+from jax.experimental.pallas import tpu as pltpu
 from jax.sharding import PartitionSpec as P
 
 TILE_LEN = 512
@@ -68,7 +70,7 @@
     return (top, total, summed)
 
 
-def local(
+def plain_local(
     text_states,
     vision_states,
     norm_gain,
@@ -140,6 +142,558 @@
     return (residual.astype(jnp.float32) + jnp.tanh(attn_gate[0]) * branch).astype(jnp.bfloat16)
 
 
+MESH = pl.DeviceIdType.MESH
+RANKS = 4
+CHUNKS = 4
+HEAD = 128
+F32, BF16 = jnp.float32, jnp.bfloat16
+
+
+def landed(ref, sem):
+    pltpu.make_async_copy(ref, ref, sem).wait()
+
+
+def fused_kernel(
+    text_ref,
+    vision_ref,
+    gain_ref,
+    qw_hbm,
+    kvw_hbm,
+    ow_hbm,
+    qgain_ref,
+    kgain_ref,
+    gate_ref,
+    counts_ref,
+    mask_ref,
+    out_ref,
+    qw,
+    kvw,
+    ow,
+    near,
+    far,
+    outer_in,
+    active,
+    text_out,
+    text_in,
+    scale_out,
+    scale_in,
+    query_part,
+    query_in,
+    query_out,
+    query_all,
+    kv_part,
+    kv_in,
+    kv_done,
+    att_out,
+    att_in,
+    rows,
+    total,
+    branch_out,
+    branch_in,
+    w_sem,
+    own_send,
+    outer_recv,
+    near_recv,
+    far_recv,
+    cross_send,
+    away_send,
+    text_send,
+    text_recv,
+    scale_send,
+    scale_recv,
+    qp_send,
+    qp_recv,
+    qa_send,
+    qa_recv,
+    kv_send,
+    kv_recv,
+    done_send,
+    done_recv,
+    att_send,
+    att_recv,
+    br_send,
+    br_recv,
+):
+    z = lax.axis_index("seq")
+    t = lax.axis_index("tensor")
+    core = lax.rem(t, 2)
+    inner = (z == 1) | (z == 2)
+    away = jnp.where(z < 2, 0, 3)
+    toward = jnp.where(z < 2, 1, 2)
+    across = 3 - z
+    row_chunk = vision_ref.shape[0] // CHUNKS
+    width = kvw.shape[2]
+
+    def remote(src, dst, send, recv, to_z, to_t):
+        return pltpu.make_async_remote_copy(
+            src_ref=src,
+            dst_ref=dst,
+            send_sem=send,
+            recv_sem=recv,
+            device_id={"seq": to_z, "tensor": to_t},
+            device_id_type=MESH,
+        )
+
+    loads = [
+        pltpu.make_async_copy(src, dst, w_sem.at[i])
+        for i, (src, dst) in enumerate(((qw_hbm, qw), (kvw_hbm, kvw), (ow_hbm, ow)))
+    ]
+    for load in loads:
+        load.start()
+
+    barrier = pltpu.get_barrier_semaphore()
+    for d in range(1, RANKS * RANKS):
+        other = lax.rem(z * RANKS + t + d, RANKS * RANKS)
+        pl.semaphore_signal(
+            barrier,
+            inc=1,
+            device_id={"seq": other // RANKS, "tensor": lax.rem(other, RANKS)},
+            device_id_type=MESH,
+        )
+
+    text = text_ref[...].astype(F32)
+    mean_sq = jnp.mean(text * text, axis=-1, keepdims=True)
+    scale_out[...] = jnp.broadcast_to(lax.rsqrt(mean_sq + EPS), scale_out.shape)
+    part = text.shape[1] // RANKS
+    half = part // 2
+    for b in range(RANKS):
+        text_out[b] = jnp.concatenate(
+            [text[:, b * part : b * part + half], text[:, b * part + half : (b + 1) * part]], axis=0
+        ).astype(BF16)
+    text_in[z] = text_out[z]
+    scale_in[z] = scale_out[...]
+
+    pl.semaphore_wait(barrier, RANKS * RANKS - 1)
+
+    def text_copies(d):
+        to = lax.rem(z + d, RANKS)
+        return (
+            remote(scale_out, scale_in.at[z], scale_send.at[d], scale_recv.at[z], to, t),
+            remote(text_out.at[to], text_in.at[z], text_send.at[d], text_recv.at[z], to, t),
+        )
+
+    for d in range(1, RANKS):
+        for copy in text_copies(d):
+            copy.start()
+
+    def chunk(ref, c):
+        return ref.at[pl.ds(pl.multiple_of(c * row_chunk, row_chunk), row_chunk)]
+
+    def own_outer(c):
+        return remote(chunk(vision_ref, c), outer_in.at[c], own_send.at[c], outer_recv.at[c], toward, t)
+
+    def own_inner(c):
+        return remote(chunk(vision_ref, c), near.at[c], own_send.at[c], near_recv.at[c], across, t)
+
+    def cross(c):
+        return remote(outer_in.at[c], far.at[c], cross_send.at[c], far_recv.at[c], across, t)
+
+    def away_near(c):
+        return remote(active.at[c], near.at[c], away_send.at[c], near_recv.at[c], away, t)
+
+    def away_far(c):
+        return remote(far.at[c], far.at[c], away_send.at[CHUNKS + c], far_recv.at[c], away, t)
+
+    @pl.when(inner)
+    def _():
+        for c in range(CHUNKS):
+            own_inner(c).start()
+
+    @pl.when(~inner)
+    def _():
+        for c in range(CHUNKS):
+            own_outer(c).start()
+
+    left = mask_ref[0, 0] == 1
+    mine = left == (z < 2)
+
+    for d in range(1, RANKS):
+        source = lax.rem(z + d, RANKS)
+        landed(scale_in.at[source], scale_recv.at[source])
+        landed(text_in.at[source], text_recv.at[source])
+    gain = gain_ref[...]
+    pieces = []
+    for b in range(RANKS):
+        raw = text_in[b].astype(F32)
+        raw = jnp.concatenate([raw[:8], raw[8:]], axis=1)
+        pieces.append(raw * scale_in[b][:, :1] * gain)
+    rows[...] = jnp.concatenate(pieces, axis=0).astype(BF16)
+    loads[0].wait()
+    tile = 512
+
+    @pl.loop(0, part // tile)
+    def _(n):
+        cols = pl.ds(pl.multiple_of(n * tile, tile), tile)
+        got = jnp.dot(rows[...], qw[:, cols], preferred_element_type=F32)
+        for b in range(RANKS):
+            query_part[b, :, cols] = got[8 * b : 8 * b + 8]
+
+    def query_copy(d):
+        to = lax.rem(z + d, RANKS)
+        return remote(query_part.at[to], query_in.at[z], qp_send.at[d], qp_recv.at[z], to, t)
+
+    for d in range(1, RANKS):
+        query_copy(d).start()
+    loads[1].wait()
+
+    def kv_copy(i, d):
+        to = lax.rem(t + d, RANKS)
+        return remote(kv_part.at[i, to], kv_in.at[i, t], kv_send.at[i, d], kv_recv.at[i, t], z, to)
+
+    def done_copy(i):
+        slot = 2 * i + core
+        return remote(
+            kv_done.at[slot], kv_done.at[slot], done_send.at[i], done_recv.at[i], z, t + 1 - 2 * core
+        )
+
+    def finish(i):
+        for d in range(1, RANKS):
+            source = lax.rem(t + d, RANKS)
+            landed(kv_in.at[i, source], kv_recv.at[i, source])
+        got = (kv_in[i, 0] + kv_in[i, 1]) + (kv_in[i, 2] + kv_in[i, 3])
+        key = root_mean_rows(got[:, :HEAD], kgain_ref[...])
+        kv_done[2 * i + core] = jnp.concatenate([key, got[:, HEAD:]], axis=1).astype(BF16)
+        done_copy(i).start()
+
+    def multiply(i):
+        chunk_rows = active[i]
+        key = jnp.dot(chunk_rows, kvw[0], preferred_element_type=F32)
+        value = jnp.dot(chunk_rows, kvw[1], preferred_element_type=F32)
+        half_rows = row_chunk // 2
+        for to in range(RANKS):
+            r, h = (to % 2) * half_rows, (to // 2) * HEAD
+            kv_part[i, to] = jnp.concatenate(
+                [key[r : r + half_rows, h : h + HEAD], value[r : r + half_rows, h : h + HEAD]], axis=1
+            )
+        kv_in[i, t] = kv_part[i, t]
+        for d in range(1, RANKS):
+            kv_copy(i, d).start()
+
+    @pl.loop(0, CHUNKS)
+    def _(c):
+        landed(near.at[c], near_recv.at[c])
+        here = pl.ds(pl.multiple_of(c * row_chunk, row_chunk), row_chunk)
+
+        @pl.when(inner)
+        def _():
+            active[c] = jnp.where(mine, vision_ref[here, :], near[c])
+            away_near(c).start()
+            landed(outer_in.at[c], outer_recv.at[c])
+            cross(c).start()
+
+        @pl.when(~inner)
+        def _():
+            active[c] = near[c]
+
+        multiply(c)
+
+        @pl.when(c > 0)
+        def _():
+            finish(c - 1)
+
+    for d in range(1, RANKS):
+        source = lax.rem(z + d, RANKS)
+        landed(query_in.at[source], qp_recv.at[source])
+    query_in[z] = query_part[z]
+    query = (query_in[0] + query_in[1]) + (query_in[2] + query_in[3])
+    heads = part // HEAD
+    for side in range(2):
+        query_out[side] = jnp.concatenate(
+            [
+                root_mean_rows(query[:, h * HEAD : (h + 1) * HEAD], qgain_ref[...])
+                for h in range(side * heads // 2, (side + 1) * heads // 2)
+            ],
+            axis=0,
+        ).astype(BF16)
+
+    def query_send(side):
+        to_t = 2 * side + z // 2
+        stays = (t == z) & (t == to_t)
+        k = lax.rem(z, 2)
+        away_copy = remote(
+            query_out.at[side], query_all.at[k], qa_send.at[side], qa_recv.at[k], t, to_t
+        )
+        here_copy = pltpu.make_async_copy(query_out.at[side], query_all.at[k], qa_recv.at[k])
+        return stays, away_copy, here_copy
+
+    def start_either(stays, away_copy, here_copy):
+        @pl.when(stays)
+        def _():
+            here_copy.start()
+
+        @pl.when(~stays)
+        def _():
+            away_copy.start()
+
+    for side in range(2):
+        start_either(*query_send(side))
+
+    @pl.loop(CHUNKS, 2 * CHUNKS)
+    def _(i):
+        c = i - CHUNKS
+        landed(far.at[c], far_recv.at[c])
+        here = pl.ds(pl.multiple_of(c * row_chunk, row_chunk), row_chunk)
+
+        @pl.when(inner)
+        def _():
+            away_far(c).start()
+            active[i] = jnp.where(mine, outer_in[c], far[c])
+
+        @pl.when(~inner)
+        def _():
+            active[i] = jnp.where(mine, vision_ref[here, :], far[c])
+
+        multiply(i)
+        finish(i - 1)
+
+    finish(2 * CHUNKS - 1)
+    for k in range(2):
+        landed(query_all.at[k], qa_recv.at[k])
+    for i in range(2 * CHUNKS):
+        slot = 2 * i + 1 - core
+        landed(kv_done.at[slot], done_recv.at[i])
+    slots = 2 * vision_ref.shape[0]
+    both = kv_done[...].reshape(slots, 2 * HEAD)
+    queries = query_all[...].reshape(2 * query_all.shape[1], HEAD)
+    scores = lax.dot_general(
+        queries, both[:, :HEAD], (((1,), (1,)), ((), ())), preferred_element_type=F32
+    ) * (HEAD**-0.5)
+    place = lax.broadcasted_iota(jnp.int32, scores.shape, 1)
+    swapped = jnp.where(place < slots // 2, place + slots // 2, place - slots // 2)
+    place = jnp.where(left, swapped, place)
+    valid = place < jnp.where(left, counts_ref[0], counts_ref[1])
+    scores = jnp.where(valid, scores, NEG)
+    top = jnp.max(scores, axis=-1, keepdims=True)
+    weights = jnp.where(valid, jnp.exp(scores - top), 0.0)
+    norm = jnp.sum(weights, axis=-1, keepdims=True)
+    high = weights.astype(BF16)
+    low = (weights - high.astype(F32)).astype(BF16)
+    value = both[:, HEAD:]
+    summed = jnp.dot(high, value, preferred_element_type=F32) + jnp.dot(
+        low, value, preferred_element_type=F32
+    )
+    att_out[...] = (summed / norm).astype(BF16)
+
+    def att_copy(d):
+        to_z = lax.rem(z + d, RANKS)
+        stays = (to_z == z) & (t == z)
+        return (
+            stays,
+            remote(att_out, att_in.at[t], att_send.at[d], att_recv.at[t], to_z, z),
+            pltpu.make_async_copy(att_out, att_in.at[t], att_recv.at[t]),
+        )
+
+    for d in (2, 1, 3):
+        stays, away_copy, here_copy = att_copy(d)
+        away_copy.start()
+    start_either(*att_copy(0))
+    loads[2].wait()
+    for source in range(RANKS):
+        landed(att_in.at[source], att_recv.at[source])
+    arrived = [att_in[source].astype(F32) for source in range(RANKS)]
+    group = 8
+    for side in range(2):
+        for j in range(group):
+            column = (side * group + j) * HEAD
+            rows[:, column : column + HEAD] = jnp.concatenate(
+                [
+                    arrived[2 * side + b // 2][(b % 2) * 64 + j * 8 : (b % 2) * 64 + j * 8 + 8]
+                    for b in range(RANKS)
+                ],
+                axis=0,
+            ).astype(BF16)
+
+    def branch_copy(n, d):
+        to = lax.rem(t + d, RANKS)
+        return remote(
+            branch_out.at[n, to], branch_in.at[n, t], br_send.at[n, d], br_recv.at[n, t], z, to
+        )
+
+    for n in range(2):
+        parts = []
+        for s in range(2):
+            start = s * half + n * tile
+            got = jnp.dot(rows[...], ow[:, start : start + tile], preferred_element_type=F32)
+            total[:, start : start + tile] = got
+            parts.append(got)
+        for to in range(RANKS):
+            branch_out[n, to] = jnp.concatenate(
+                [got[8 * to : 8 * to + 8] for got in parts], axis=0
+            ).astype(BF16)
+        for d in (2, 1, 3):
+            branch_copy(n, d).start()
+
+    gate = jnp.tanh(jnp.full((8, tile), gate_ref[0], F32))
+    residual = text_in[t].astype(F32)
+    own_rows = pl.ds(pl.multiple_of(8 * t, 8), 8)
+    for n in range(2):
+        for d in range(1, RANKS):
+            source = lax.rem(t + d, RANKS)
+            landed(branch_in.at[n, source], br_recv.at[n, source])
+        others = []
+        for d in range(1, RANKS):
+            others.append(branch_in[n, lax.rem(t + d, RANKS)].astype(F32))
+        other = (others[0] + others[1]) + others[2]
+        for s in range(2):
+            start = s * half + n * tile
+            branch = total[own_rows, start : start + tile] + other[8 * s : 8 * s + 8]
+            base = residual[8 * s : 8 * s + 8, n * tile : (n + 1) * tile]
+            out_ref[:, start : start + tile] = (base + gate * branch).astype(BF16)
+
+    for d in range(1, RANKS):
+        for copy in text_copies(d):
+            copy.wait_send()
+        query_copy(d).wait_send()
+        att_copy(d)[1].wait_send()
+        for n in range(2):
+            branch_copy(n, d).wait_send()
+    stays, away_copy, here_copy = att_copy(0)
+
+    @pl.when(~stays)
+    def _():
+        away_copy.wait_send()
+
+    for side in range(2):
+        q_stays, q_away, q_here = query_send(side)
+
+        @pl.when(~q_stays)
+        def _():
+            q_away.wait_send()
+
+    @pl.loop(0, CHUNKS)
+    def _(c):
+        own_inner(c).wait_send()
+
+        @pl.when(inner)
+        def _():
+            cross(c).wait_send()
+            away_near(c).wait_send()
+            away_far(c).wait_send()
+
+    @pl.loop(0, 2 * CHUNKS)
+    def _(i):
+        for d in range(1, RANKS):
+            kv_copy(i, d).wait_send()
+        done_copy(i).wait_send()
+
+
+def fused_fits(text_states, vision_states, query_weight, key_value_weight, out_weight, query_gain, tile_counts, tile_mask):
+    return (
+        lax.axis_size("seq") == RANKS
+        and lax.axis_size("tensor") == RANKS
+        and tile_mask.shape == (1, 2)
+        and tile_counts.shape == (2,)
+        and text_states.shape == (8, 8192)
+        and vision_states.shape == (256, 2048)
+        and query_weight.shape == (2048, 2048)
+        and out_weight.shape == (2048, 2048)
+        and key_value_weight.shape == (2, 2048, 256)
+        and query_gain.shape == (HEAD,)
+    )
+
+
+def fused_local(
+    text_states,
+    vision_states,
+    norm_gain,
+    query_weight,
+    key_value_weight,
+    out_weight,
+    query_gain,
+    key_norm_gain,
+    attn_gate,
+    tile_counts,
+    tile_mask,
+):
+    part = query_weight.shape[0]
+    tokens, slots = text_states.shape[0], vision_states.shape[0]
+    chunk = slots // CHUNKS
+    z = lax.axis_index("seq")
+    gain = lax.dynamic_slice_in_dim(norm_gain, z * part, part).astype(F32).reshape(1, part)
+    vmem = pl.BlockSpec(memory_space=pltpu.VMEM)
+    smem = pl.BlockSpec(memory_space=pltpu.SMEM)
+    hbm = pl.BlockSpec(memory_space=pl.ANY)
+    block = pltpu.VMEM((CHUNKS, chunk, part), BF16)
+    dma = pltpu.SemaphoreType.DMA
+    return pl.pallas_call(
+        fused_kernel,
+        out_shape=jax.ShapeDtypeStruct((tokens, part), BF16),
+        in_specs=[vmem, vmem, vmem, hbm, hbm, hbm, vmem, vmem, smem, smem, smem],
+        out_specs=vmem,
+        scratch_shapes=[
+            pltpu.VMEM(query_weight.shape, BF16),
+            pltpu.VMEM(key_value_weight.shape, BF16),
+            pltpu.VMEM(out_weight.shape, BF16),
+            block,
+            block,
+            block,
+            pltpu.VMEM((2 * CHUNKS, chunk, part), BF16),
+            pltpu.VMEM((RANKS, 16, part // 2), BF16),
+            pltpu.VMEM((RANKS, 16, part // 2), BF16),
+            pltpu.VMEM((8, HEAD), F32),
+            pltpu.VMEM((RANKS, 8, HEAD), F32),
+            pltpu.VMEM((RANKS, 8, part), F32),
+            pltpu.VMEM((RANKS, 8, part), F32),
+            pltpu.VMEM((2, 64, HEAD), BF16),
+            pltpu.VMEM((2, 64, HEAD), BF16),
+            pltpu.VMEM((2 * CHUNKS, RANKS, chunk // 2, 2 * HEAD), F32),
+            pltpu.VMEM((2 * CHUNKS, RANKS, chunk // 2, 2 * HEAD), F32),
+            pltpu.VMEM((4 * CHUNKS, chunk // 2, 2 * HEAD), BF16),
+            pltpu.VMEM((128, HEAD), BF16),
+            pltpu.VMEM((RANKS, 128, HEAD), BF16),
+            pltpu.VMEM((32, part), BF16),
+            pltpu.VMEM((32, part), F32),
+            pltpu.VMEM((2, RANKS, 16, 512), BF16),
+            pltpu.VMEM((2, RANKS, 16, 512), BF16),
+            dma((3,)),
+            dma((CHUNKS,)),
+            dma((CHUNKS,)),
+            dma((CHUNKS,)),
+            dma((CHUNKS,)),
+            dma((CHUNKS,)),
+            dma((2 * CHUNKS,)),
+            dma((RANKS,)),
+            dma((RANKS,)),
+            dma((RANKS,)),
+            dma((RANKS,)),
+            dma((RANKS,)),
+            dma((RANKS,)),
+            dma((2,)),
+            dma((2,)),
+            dma((2 * CHUNKS, RANKS)),
+            dma((2 * CHUNKS, RANKS)),
+            dma((2 * CHUNKS,)),
+            dma((2 * CHUNKS,)),
+            dma((RANKS,)),
+            dma((RANKS,)),
+            dma((2, RANKS)),
+            dma((2, RANKS)),
+        ],
+        compiler_params=pltpu.CompilerParams(
+            collective_id=0, has_side_effects=True, vmem_limit_bytes=56 * 1024 * 1024
+        ),
+    )(
+        text_states,
+        vision_states,
+        gain,
+        query_weight,
+        key_value_weight,
+        out_weight,
+        query_gain.reshape(1, HEAD),
+        key_norm_gain.reshape(1, HEAD),
+        attn_gate,
+        tile_counts,
+        tile_mask,
+    )
+
+
+def local(*args):
+    text, vision, _, query_weight, kv_weight, out_weight, query_gain, _, _, counts, mask = args
+    if fused_fits(text, vision, query_weight, kv_weight, out_weight, query_gain, counts, mask):
+        return fused_local(*args)
+    return plain_local(*args)
+
+
 def solution(mesh):
     return jax.shard_map(
         local,

time: 290 us -> 90.9 us (0.31)
  waiting for transfers between devices: 179 us -> 0 us
  Pallas kernels: 0 us -> 87.3 us
  blocking collectives: 52.7 us -> 0 us
  matrix products: 20.5 us -> 0 us
  between operations: 14 us -> 0.66 us
  local copies, waits for them, and re-layouts: 11.5 us -> 1.38 us
  other arithmetic: 7.69 us -> 1.29 us
  starting transfers between devices: 3.51 us -> 0 us
    all_gather x2 -> x0, waiting for transfers between devices: 134 us -> none  [the longest x1 131 us: local(): lax.all_gather(key_value_weight, 'seq', axis=2, tiled=True)]
    pallas_call x0 -> x1, Pallas kernels: none -> 87.3 us  [fused_local(): pl.pallas_call(fused_kernel, out_shape=jax.ShapeDtypeStruct((tokens, part...]
    all_gather x3 -> x0, blocking collectives: 40.5 us -> none  [the longest x2 28.2 us: combined_all(): gathered = jax.tree.map(lambda a: lax.all_gather(a, axis), part)]
    reduce_scatter x3 -> x0, waiting for transfers between devices: 40.2 us -> none  [the longest x1 18.1 us: local(): lax.psum_scatter(kv_full, 'tensor', scatter_dimension=2, tiled=True)]
    dot_general x6 -> x0, matrix products: 20.5 us -> none  [the longest x1 7.17 us: local(): jnp.einsum('vd,jdc->jvc', vision_states, lax.all_gather(key_value_weight,...]
    all_to_all x1 -> x0, blocking collectives: 12.2 us -> none  [local(): lax.all_to_all(normed, 'seq', split_axis=1, concat_axis=0, tiled=True)]
    all_to_all x1 -> x0, waiting for transfers between devices: 5.54 us -> none  [local(): lax.all_to_all(text_states, 'seq', split_axis=1, concat_axis=0, tiled=True)]
    convert_element_type x5 -> x0, other arithmetic: 4.27 us -> none  [the longest x1 1.46 us: local(): (residual.astype(jnp.float32) + jnp.tanh(attn_gate[0]) * branch).astype(j...]
  transfers between devices with their start and end apart: 6 -> 0, of which waited for: 6 -> 0; matrix products, arithmetic and copies ran while one was open for 7% -> 0% of each run, Pallas kernels for 0% -> 0%
where the time goes in v1:
time: 90.9 us; the launch traced here: 90.6 us
  Pallas kernels  87.3 us (96%)
  local copies, waits for them, and re-layouts  1.38 us (2%)
  other arithmetic  1.29 us (1%)
    pallas_call x1, Pallas kernels, fused_local(): pl.pallas_call(fused_kernel, out_shape=jax.ShapeDtypeStruct((tokens, part...  87.3 us

profile of v1, /device:TPU:0, one launch (start us, length us, event | category | flops | bytes accessed | tf_op | source)
XLA Modules:
  0.0 90.6 jit_solution(15654003301187622346)
XLA Ops:
  0.7 1.3 %dynamic-slice_convert_fusion = f32[2048]{0:T(1024)} fusion(bf16[8192]{0:T(1024)(128)(2,1)} %param.13, s32[]{:T(128)S(6)} %select_n.3), kind=kLoop, calls=%fused_computation | loop fusion | flops 2048 | bytes 12292 | tf_op jit(solution)/shard_map/reshape | solution.py:612
  1.9 87.3 %shard_map.109 = bf16[8,2048]{1,0:T(8,128)(2,1)} custom-call(bf16[8,8192]{1,0:T(8,128)(2,1)} %text_ref.1, bf16[256,2048]{1,0:T(8,128)(2,1)} %vision_ref.1, f32[1,2048]{1,0:T(1,128)} %bitcast.3, bf16[2048,2048]{1,0:T(8,128)(2,1)} %qw_hbm.1, bf16[2,2048,256]{2,1,0:T(8,128)(2,1)} %kvw_hbm.1, bf16[2048,2048]{1,0:T(8,128)(2,1)} %ow_hbm.1, f32[1,128]{1,0:T(1,128)} %bitcast.4, ...), custom_call_target="tpu_custom_call" | custom-call | tf_op jit(solution)/shard_map/pallas_call | solution.py:618
  89.3 1.4 %copy.14 = bf16[8,2048]{1,0:T(8,128)(2,1)} copy(bf16[8,2048]{1,0:T(8,128)(2,1)} %shard_map.109) | data formatting | bytes 65536

commit v2 on v1

--- a/solution.py
+++ b/solution.py
@@ -145,6 +145,9 @@
 MESH = pl.DeviceIdType.MESH
 RANKS = 4
 CHUNKS = 4
+SUBS = 2
+SENDS = CHUNKS * SUBS
+AHEAD = 3
 HEAD = 128
 F32, BF16 = jnp.float32, jnp.bfloat16
 
@@ -179,6 +182,10 @@
     scale_in,
     query_part,
     query_in,
+    mid_out,
+    mid_in,
+    last_out,
+    last_in,
     query_out,
     query_all,
     kv_part,
@@ -203,6 +210,8 @@
     scale_recv,
     qp_send,
     qp_recv,
+    mid_sem,
+    last_sem,
     qa_send,
     qa_recv,
     kv_send,
@@ -222,7 +231,7 @@
     toward = jnp.where(z < 2, 1, 2)
     across = 3 - z
     row_chunk = vision_ref.shape[0] // CHUNKS
-    width = kvw.shape[2]
+    sub_rows = row_chunk // SUBS
 
     def remote(src, dst, send, recv, to_z, to_t):
         return pltpu.make_async_remote_copy(
@@ -276,64 +285,87 @@
         for copy in text_copies(d):
             copy.start()
 
-    def chunk(ref, c):
-        return ref.at[pl.ds(pl.multiple_of(c * row_chunk, row_chunk), row_chunk)]
-
-    def own_outer(c):
-        return remote(chunk(vision_ref, c), outer_in.at[c], own_send.at[c], outer_recv.at[c], toward, t)
-
-    def own_inner(c):
-        return remote(chunk(vision_ref, c), near.at[c], own_send.at[c], near_recv.at[c], across, t)
-
-    def cross(c):
-        return remote(outer_in.at[c], far.at[c], cross_send.at[c], far_recv.at[c], across, t)
-
-    def away_near(c):
-        return remote(active.at[c], near.at[c], away_send.at[c], near_recv.at[c], away, t)
-
-    def away_far(c):
-        return remote(far.at[c], far.at[c], away_send.at[CHUNKS + c], far_recv.at[c], away, t)
+    def rows_of(u):
+        return pl.ds(pl.multiple_of(u * sub_rows, sub_rows), sub_rows)
+
+    def sub(ref, u):
+        return ref.at[rows_of(u)]
+
+    def own_outer(u):
+        return remote(
+            sub(vision_ref, u), sub(outer_in, u), own_send.at[u], outer_recv.at[u], toward, t
+        )
+
+    def own_inner(u):
+        return remote(sub(vision_ref, u), sub(near, u), own_send.at[u], near_recv.at[u], across, t)
+
+    def cross(u):
+        return remote(sub(outer_in, u), sub(far, u), cross_send.at[u], far_recv.at[u], across, t)
+
+    def away_near(u):
+        return remote(sub(active, u), sub(near, u), away_send.at[u], near_recv.at[u], away, t)
+
+    def away_far(u):
+        return remote(sub(far, u), sub(far, u), away_send.at[SENDS + u], far_recv.at[u], away, t)
+
+    def send_across(m):
+        @pl.when(m < SENDS)
+        def _():
+            own_inner(m).start()
+
+        @pl.when((m >= SENDS) & (m < 2 * SENDS))
+        def _():
+            u = m - SENDS
+            landed(sub(outer_in, u), outer_recv.at[u])
+            cross(u).start()
 
     @pl.when(inner)
     def _():
-        for c in range(CHUNKS):
-            own_inner(c).start()
+        for u in range(AHEAD):
+            own_inner(u).start()
 
     @pl.when(~inner)
     def _():
-        for c in range(CHUNKS):
-            own_outer(c).start()
+        for u in range(SENDS):
+            own_outer(u).start()
 
     left = mask_ref[0, 0] == 1
     mine = left == (z < 2)
 
-    for d in range(1, RANKS):
-        source = lax.rem(z + d, RANKS)
-        landed(scale_in.at[source], scale_recv.at[source])
-        landed(text_in.at[source], text_recv.at[source])
-    gain = gain_ref[...]
-    pieces = []
-    for b in range(RANKS):
-        raw = text_in[b].astype(F32)
-        raw = jnp.concatenate([raw[:8], raw[8:]], axis=1)
-        pieces.append(raw * scale_in[b][:, :1] * gain)
-    rows[...] = jnp.concatenate(pieces, axis=0).astype(BF16)
-    loads[0].wait()
     tile = 512
 
-    @pl.loop(0, part // tile)
-    def _(n):
-        cols = pl.ds(pl.multiple_of(n * tile, tile), tile)
+    def take_text():
+        for d in range(1, RANKS):
+            source = lax.rem(z + d, RANKS)
+            landed(scale_in.at[source], scale_recv.at[source])
+            landed(text_in.at[source], text_recv.at[source])
+        gain = gain_ref[pl.ds(pl.multiple_of(z * part, part), part)].astype(F32).reshape(1, part)
+        pieces = []
+        for b in range(RANKS):
+            raw = text_in[b].astype(F32)
+            raw = jnp.concatenate([raw[:8], raw[8:]], axis=1)
+            pieces.append(raw * scale_in[b][:, :1] * gain)
+        rows[...] = jnp.concatenate(pieces, axis=0).astype(BF16)
+        loads[0].wait()
+
+    def query_tile(n):
+        cols = slice(n * tile, (n + 1) * tile)
         got = jnp.dot(rows[...], qw[:, cols], preferred_element_type=F32)
         for b in range(RANKS):
             query_part[b, :, cols] = got[8 * b : 8 * b + 8]
 
-    def query_copy(d):
-        to = lax.rem(z + d, RANKS)
-        return remote(query_part.at[to], query_in.at[z], qp_send.at[d], qp_recv.at[z], to, t)
-
-    for d in range(1, RANKS):
-        query_copy(d).start()
+    outer_blocks = (toward, 3 - toward, 3 - z)
+
+    def query_inward(n):
+        b = outer_blocks[n]
+        return remote(query_part.at[b], query_in.at[b], qp_send.at[n], qp_recv.at[b], toward, t)
+
+    def query_across():
+        return remote(mid_out, mid_in, mid_sem.at[0], mid_sem.at[1], across, t)
+
+    def query_outward():
+        return remote(last_out, last_in, last_sem.at[0], last_sem.at[1], away, t)
+
     loads[1].wait()
 
     def kv_copy(i, d):
@@ -356,7 +388,7 @@
         done_copy(i).start()
 
     def multiply(i):
-        chunk_rows = active[i]
+        chunk_rows = active[pl.ds(pl.multiple_of(i * row_chunk, row_chunk), row_chunk), :]
         key = jnp.dot(chunk_rows, kvw[0], preferred_element_type=F32)
         value = jnp.dot(chunk_rows, kvw[1], preferred_element_type=F32)
         half_rows = row_chunk // 2
@@ -371,19 +403,20 @@
 
     @pl.loop(0, CHUNKS)
     def _(c):
-        landed(near.at[c], near_recv.at[c])
-        here = pl.ds(pl.multiple_of(c * row_chunk, row_chunk), row_chunk)
-
-        @pl.when(inner)
-        def _():
-            active[c] = jnp.where(mine, vision_ref[here, :], near[c])
-            away_near(c).start()
-            landed(outer_in.at[c], outer_recv.at[c])
-            cross(c).start()
-
-        @pl.when(~inner)
-        def _():
-            active[c] = near[c]
+        for s in range(SUBS):
+            u = c * SUBS + s
+            here = rows_of(u)
+            landed(sub(near, u), near_recv.at[u])
+
+            @pl.when(inner)
+            def _():
+                active[here, :] = jnp.where(mine, vision_ref[here, :], near[here, :])
+                away_near(u).start()
+                send_across(u + AHEAD)
+
+            @pl.when(~inner)
+            def _():
+                active[here, :] = near[here, :]
 
         multiply(c)
 
@@ -391,20 +424,43 @@
         def _():
             finish(c - 1)
 
-    for d in range(1, RANKS):
-        source = lax.rem(z + d, RANKS)
-        landed(query_in.at[source], qp_recv.at[source])
-    query_in[z] = query_part[z]
-    query = (query_in[0] + query_in[1]) + (query_in[2] + query_in[3])
+        @pl.when(c == 1)
+        def _():
+            take_text()
+            query_tile(0)
+            query_tile(1)
+
+        @pl.when(c == 2)
+        def _():
+            query_tile(2)
+            query_tile(3)
+
+            @pl.when(~inner)
+            def _():
+                for n in range(3):
+                    query_inward(n).start()
+
+        @pl.when((c == 3) & inner)
+        def _():
+            for b in (z, across, 3 - away):
+                landed(query_in.at[b], qp_recv.at[b])
+            for n, b in enumerate((across, 3 - away)):
+                mid_out[n] = query_part[b] + query_in[b]
+            query_across().start()
+
     heads = part // HEAD
-    for side in range(2):
-        query_out[side] = jnp.concatenate(
-            [
-                root_mean_rows(query[:, h * HEAD : (h + 1) * HEAD], qgain_ref[...])
-                for h in range(side * heads // 2, (side + 1) * heads // 2)
-            ],
-            axis=0,
-        ).astype(BF16)
+
+    def take_query(query):
+        for side in range(2):
+            query_out[side] = jnp.concatenate(
+                [
+                    root_mean_rows(query[:, h * HEAD : (h + 1) * HEAD], qgain_ref[...])
+                    for h in range(side * heads // 2, (side + 1) * heads // 2)
+                ],
+                axis=0,
+            ).astype(BF16)
+        for side in range(2):
+            start_either(*query_send(side))
 
     def query_send(side):
         to_t = 2 * side + z // 2
@@ -425,26 +481,38 @@
         def _():
             away_copy.start()
 
-    for side in range(2):
-        start_either(*query_send(side))
-
     @pl.loop(CHUNKS, 2 * CHUNKS)
     def _(i):
-        c = i - CHUNKS
-        landed(far.at[c], far_recv.at[c])
-        here = pl.ds(pl.multiple_of(c * row_chunk, row_chunk), row_chunk)
-
-        @pl.when(inner)
-        def _():
-            away_far(c).start()
-            active[i] = jnp.where(mine, outer_in[c], far[c])
-
-        @pl.when(~inner)
-        def _():
-            active[i] = jnp.where(mine, vision_ref[here, :], far[c])
+        for s in range(SUBS):
+            u = (i - CHUNKS) * SUBS + s
+            here = rows_of(u)
+            to = rows_of(u + SENDS)
+            landed(sub(far, u), far_recv.at[u])
+
+            @pl.when(inner)
+            def _():
+                away_far(u).start()
+                send_across(u + SENDS + AHEAD)
+                active[to, :] = jnp.where(mine, outer_in[here, :], far[here, :])
+
+            @pl.when(~inner)
+            def _():
+                active[to, :] = jnp.where(mine, vision_ref[here, :], far[here, :])
 
         multiply(i)
         finish(i - 1)
+
+        @pl.when((i == CHUNKS + 1) & inner)
+        def _():
+            landed(mid_in, mid_sem.at[1])
+            last_out[...] = query_part[away] + mid_in[1]
+            query_outward().start()
+            take_query((query_part[z] + query_in[z]) + mid_in[0])
+
+        @pl.when((i == CHUNKS + 2) & ~inner)
+        def _():
+            landed(last_in, last_sem.at[1])
+            take_query(query_part[z] + last_in[...])
 
     finish(2 * CHUNKS - 1)
     for k in range(2):
@@ -543,7 +611,6 @@
     for d in range(1, RANKS):
         for copy in text_copies(d):
             copy.wait_send()
-        query_copy(d).wait_send()
         att_copy(d)[1].wait_send()
         for n in range(2):
             branch_copy(n, d).wait_send()
@@ -560,15 +627,25 @@
         def _():
             q_away.wait_send()
 
-    @pl.loop(0, CHUNKS)
-    def _(c):
-        own_inner(c).wait_send()
+    @pl.when(inner)
+    def _():
+        query_across().wait_send()
+        query_outward().wait_send()
+
+    @pl.when(~inner)
+    def _():
+        for n in range(3):
+            query_inward(n).wait_send()
+
+    @pl.loop(0, SENDS)
+    def _(u):
+        own_inner(u).wait_send()
 
         @pl.when(inner)
         def _():
-            cross(c).wait_send()
-            away_near(c).wait_send()
-            away_far(c).wait_send()
+            cross(u).wait_send()
+            away_near(u).wait_send()
+            away_far(u).wait_send()
 
     @pl.loop(0, 2 * CHUNKS)
     def _(i):
@@ -608,12 +685,10 @@
     part = query_weight.shape[0]
     tokens, slots = text_states.shape[0], vision_states.shape[0]
     chunk = slots // CHUNKS
-    z = lax.axis_index("seq")
-    gain = lax.dynamic_slice_in_dim(norm_gain, z * part, part).astype(F32).reshape(1, part)
     vmem = pl.BlockSpec(memory_space=pltpu.VMEM)
     smem = pl.BlockSpec(memory_space=pltpu.SMEM)
     hbm = pl.BlockSpec(memory_space=pl.ANY)
-    block = pltpu.VMEM((CHUNKS, chunk, part), BF16)
+    block = pltpu.VMEM((slots, part), BF16)
     dma = pltpu.SemaphoreType.DMA
     return pl.pallas_call(
         fused_kernel,
@@ -627,13 +702,17 @@
             block,
             block,
             block,
-            pltpu.VMEM((2 * CHUNKS, chunk, part), BF16),
+            pltpu.VMEM((2 * slots, part), BF16),
             pltpu.VMEM((RANKS, 16, part // 2), BF16),
             pltpu.VMEM((RANKS, 16, part // 2), BF16),
             pltpu.VMEM((8, HEAD), F32),
             pltpu.VMEM((RANKS, 8, HEAD), F32),
             pltpu.VMEM((RANKS, 8, part), F32),
             pltpu.VMEM((RANKS, 8, part), F32),
+            pltpu.VMEM((2, 8, part), F32),
+            pltpu.VMEM((2, 8, part), F32),
+            pltpu.VMEM((8, part), F32),
+            pltpu.VMEM((8, part), F32),
             pltpu.VMEM((2, 64, HEAD), BF16),
             pltpu.VMEM((2, 64, HEAD), BF16),
             pltpu.VMEM((2 * CHUNKS, RANKS, chunk // 2, 2 * HEAD), F32),
@@ -646,18 +725,20 @@
             pltpu.VMEM((2, RANKS, 16, 512), BF16),
             pltpu.VMEM((2, RANKS, 16, 512), BF16),
             dma((3,)),
-            dma((CHUNKS,)),
-            dma((CHUNKS,)),
-            dma((CHUNKS,)),
-            dma((CHUNKS,)),
-            dma((CHUNKS,)),
-            dma((2 * CHUNKS,)),
+            dma((SENDS,)),
+            dma((SENDS,)),
+            dma((SENDS,)),
+            dma((SENDS,)),
+            dma((SENDS,)),
+            dma((2 * SENDS,)),
             dma((RANKS,)),
             dma((RANKS,)),
             dma((RANKS,)),
             dma((RANKS,)),
             dma((RANKS,)),
             dma((RANKS,)),
+            dma((2,)),
+            dma((2,)),
             dma((2,)),
             dma((2,)),
             dma((2 * CHUNKS, RANKS)),
@@ -675,7 +756,7 @@
     )(
         text_states,
         vision_states,
-        gain,
+        norm_gain,
         query_weight,
         key_value_weight,
         out_weight,

time: 90.9 us -> 84.7 us (0.932)
  Pallas kernels: 87.3 us -> 82.5 us
  other arithmetic: 1.29 us -> 0 us
    pallas_call x1, Pallas kernels: 87.3 us -> 82.5 us  [fused_local(): pl.pallas_call(fused_kernel, out_shape=jax.ShapeDtypeStruct((tokens, part...]
    reshape x1 -> x0, other arithmetic: 1.29 us -> none  [fused_local(): lax.dynamic_slice_in_dim(norm_gain, z * part, part).astype(F32)]
where the time goes in v2:
time: 84.7 us; the launch traced here: 84.5 us
  Pallas kernels  82.5 us (97%)
  local copies, waits for them, and re-layouts  1.38 us (2%)
    pallas_call x1, Pallas kernels, fused_local(): pl.pallas_call(fused_kernel, out_shape=jax.ShapeDtypeStruct((tokens, part...  82.5 us

profile of v2, /device:TPU:0, one launch (start us, length us, event | category | flops | bytes accessed | tf_op | source)
XLA Modules:
  0.0 84.5 jit_solution(4281561804926992242)
XLA Ops:
  0.7 82.5 %shard_map.109 = bf16[8,2048]{1,0:T(8,128)(2,1)} custom-call(bf16[8,8192]{1,0:T(8,128)(2,1)} %text_ref.1, bf16[256,2048]{1,0:T(8,128)(2,1)} %vision_ref.1, bf16[8192]{0:T(1024)(128)(2,1)} %gain_ref.1, bf16[2048,2048]{1,0:T(8,128)(2,1)} %qw_hbm.1, bf16[2,2048,256]{2,1,0:T(8,128)(2,1)} %kvw_hbm.1, bf16[2048,2048]{1,0:T(8,128)(2,1)} %ow_hbm.1, ...), custom_call_target="tpu_custom_call" | custom-call | tf_op jit(solution)/shard_map/pallas_call | solution.py:693
  83.1 1.4 %copy.14 = bf16[8,2048]{1,0:T(8,128)(2,1)} copy(bf16[8,2048]{1,0:T(8,128)(2,1)} %shard_map.109) | data formatting | bytes 65536

commit v3 on v2

--- a/solution.py
+++ b/solution.py
@@ -206,6 +206,7 @@
     away_send,
     text_send,
     text_recv,
+    spread_send,
     scale_send,
     scale_recv,
     qp_send,
@@ -265,10 +266,13 @@
     scale_out[...] = jnp.broadcast_to(lax.rsqrt(mean_sq + EPS), scale_out.shape)
     part = text.shape[1] // RANKS
     half = part // 2
+    piece = half // RANKS
     for b in range(RANKS):
-        text_out[b] = jnp.concatenate(
-            [text[:, b * part : b * part + half], text[:, b * part + half : (b + 1) * part]], axis=0
-        ).astype(BF16)
+        for p in range(RANKS):
+            low, high = b * part + p * piece, b * part + half + p * piece
+            text_out[b, p] = jnp.concatenate(
+                [text[:, low : low + piece], text[:, high : high + piece]], axis=0
+            ).astype(BF16)
     text_in[z] = text_out[z]
     scale_in[z] = scale_out[...]
 
@@ -278,7 +282,9 @@
         to = lax.rem(z + d, RANKS)
         return (
             remote(scale_out, scale_in.at[z], scale_send.at[d], scale_recv.at[z], to, t),
-            remote(text_out.at[to], text_in.at[z], text_send.at[d], text_recv.at[z], to, t),
+            remote(
+                text_out.at[to, t], text_in.at[z, t], text_send.at[d], text_recv.at[z, t], to, t
+            ),
         )
 
     for d in range(1, RANKS):
@@ -334,17 +340,33 @@
 
     tile = 512
 
+    def spread_copy(d, e):
+        b, to = lax.rem(z + d, RANKS), lax.rem(t + e, RANKS)
+        block = text_in.at[b, t]
+        return remote(block, block, spread_send.at[d, e], text_recv.at[b, t], z, to)
+
+    def spread_text():
+        for d in range(1, RANKS):
+            source = lax.rem(z + d, RANKS)
+            landed(text_in.at[source, t], text_recv.at[source, t])
+            for e in range(1, RANKS):
+                spread_copy(d, e).start()
+
+    def whole(b):
+        raw = jnp.concatenate([text_in[b, p].astype(F32) for p in range(RANKS)], axis=1)
+        return jnp.concatenate([raw[:8], raw[8:]], axis=1)
+
     def take_text():
         for d in range(1, RANKS):
             source = lax.rem(z + d, RANKS)
             landed(scale_in.at[source], scale_recv.at[source])
-            landed(text_in.at[source], text_recv.at[source])
+            for e in range(1, RANKS):
+                p = lax.rem(t + e, RANKS)
+                landed(text_in.at[source, p], text_recv.at[source, p])
         gain = gain_ref[pl.ds(pl.multiple_of(z * part, part), part)].astype(F32).reshape(1, part)
         pieces = []
         for b in range(RANKS):
-            raw = text_in[b].astype(F32)
-            raw = jnp.concatenate([raw[:8], raw[8:]], axis=1)
-            pieces.append(raw * scale_in[b][:, :1] * gain)
+            pieces.append(whole(b) * scale_in[b][:, :1] * gain)
         rows[...] = jnp.concatenate(pieces, axis=0).astype(BF16)
         loads[0].wait()
 
@@ -423,6 +445,10 @@
         @pl.when(c > 0)
         def _():
             finish(c - 1)
+
+        @pl.when(c == 0)
+        def _():
+            spread_text()
 
         @pl.when(c == 1)
         def _():
@@ -592,7 +618,7 @@
             branch_copy(n, d).start()
 
     gate = jnp.tanh(jnp.full((8, tile), gate_ref[0], F32))
-    residual = text_in[t].astype(F32)
+    residual = whole(t)
     own_rows = pl.ds(pl.multiple_of(8 * t, 8), 8)
     for n in range(2):
         for d in range(1, RANKS):
@@ -605,12 +631,14 @@
         for s in range(2):
             start = s * half + n * tile
             branch = total[own_rows, start : start + tile] + other[8 * s : 8 * s + 8]
-            base = residual[8 * s : 8 * s + 8, n * tile : (n + 1) * tile]
+            base = residual[:, start : start + tile]
             out_ref[:, start : start + tile] = (base + gate * branch).astype(BF16)
 
     for d in range(1, RANKS):
         for copy in text_copies(d):
             copy.wait_send()
+        for e in range(1, RANKS):
+            spread_copy(d, e).wait_send()
         att_copy(d)[1].wait_send()
         for n in range(2):
             branch_copy(n, d).wait_send()
@@ -703,8 +731,8 @@
             block,
             block,
             pltpu.VMEM((2 * slots, part), BF16),
-            pltpu.VMEM((RANKS, 16, part // 2), BF16),
-            pltpu.VMEM((RANKS, 16, part // 2), BF16),
+            pltpu.VMEM((RANKS, RANKS, 16, part // 8), BF16),
+            pltpu.VMEM((RANKS, RANKS, 16, part // 8), BF16),
             pltpu.VMEM((8, HEAD), F32),
             pltpu.VMEM((RANKS, 8, HEAD), F32),
             pltpu.VMEM((RANKS, 8, part), F32),
@@ -732,7 +760,8 @@
             dma((SENDS,)),
             dma((2 * SENDS,)),
             dma((RANKS,)),
-            dma((RANKS,)),
+            dma((RANKS, RANKS)),
+            dma((RANKS, RANKS)),
             dma((RANKS,)),
             dma((RANKS,)),
             dma((RANKS,)),

time: 84.7 us -> 82.9 us (0.979)
  Pallas kernels: 82.5 us -> 80.6 us
    pallas_call x1, Pallas kernels: 82.5 us -> 80.6 us  [fused_local(): pl.pallas_call(fused_kernel, out_shape=jax.ShapeDtypeStruct((tokens, part...]
where the time goes in v3:
time: 82.9 us; the launch traced here: 82.7 us
  Pallas kernels  80.6 us (97%)
  local copies, waits for them, and re-layouts  1.38 us (2%)
    pallas_call x1, Pallas kernels, fused_local(): pl.pallas_call(fused_kernel, out_shape=jax.ShapeDtypeStruct((tokens, part...  80.6 us

profile of v3, /device:TPU:0, one launch (start us, length us, event | category | flops | bytes accessed | tf_op | source)
XLA Modules:
  0.0 82.7 jit_solution(48345975393872605)
XLA Ops:
  0.7 80.6 %shard_map.109 = bf16[8,2048]{1,0:T(8,128)(2,1)} custom-call(bf16[8,8192]{1,0:T(8,128)(2,1)} %text_ref.1, bf16[256,2048]{1,0:T(8,128)(2,1)} %vision_ref.1, bf16[8192]{0:T(1024)(128)(2,1)} %gain_ref.1, bf16[2048,2048]{1,0:T(8,128)(2,1)} %qw_hbm.1, bf16[2,2048,256]{2,1,0:T(8,128)(2,1)} %kvw_hbm.1, bf16[2048,2048]{1,0:T(8,128)(2,1)} %ow_hbm.1, ...), custom_call_target="tpu_custom_call" | custom-call | tf_op jit(solution)/shard_map/pallas_call | solution.py:721
  81.3 1.4 %copy.14 = bf16[8,2048]{1,0:T(8,128)(2,1)} copy(bf16[8,2048]{1,0:T(8,128)(2,1)} %shard_map.109) | data formatting | bytes 65536
